TPU v7x, 32 devices: a whole 2x2x4 slice. The times are simulated.
32 devices in a mesh: stream: 8 (over z, x), tensor: 4 (over y, core).
Axes of the slice: x: 2, y: 2, z: 4, core: 2. Of those that a mesh axis runs over, the one named last changes fastest.
Arguments:
- hidden: bfloat16 [512, 8192], P('stream', 'tensor'), may hold values from -600 to 600
- norm_gain: bfloat16 [8192], replicated, may hold values from 0.099609375 to 1.8984375
- head_weight: bfloat16 [8192, 128256], P(None, ('stream', 'tensor')), may hold values from -32 to 32
- floor_counts: int32 [128256], P(('stream', 'tensor')), may hold values from 1 to 7
- totals: int32 [512], replicated, may hold values from 1048576 to 4194304
- targets: int32 [512], replicated, may hold values from 0 to 128255
Outputs:
- cumulative: float32 [512, 128256], P(None, ('stream', 'tensor'))
- code_bits: float32 [512], replicated
All inputs are finite; a program needn't handle non-finite values.
Results may differ from a plain program's by a relative error of at most 0.0003.
The roundings to bfloat16 on the way count: a program that leaves them out, or rounds other values in their place, can miss the bound.
Values may be sent and summed in bfloat16 or wider, within the bound.
A program may use at most 192 MiB of HBM per device.

v0:
```python
import jax
import jax.numpy as jnp
from jax import lax
from jax.sharding import PartitionSpec as P

epsilon = 1e-05


def prefix(value, axis, join, neutral):
    count, mine = (lax.axis_size(axis), lax.axis_index(axis))
    pieces = lax.all_gather(value, axis)
    subtotal = jnp.full_like(value, 0) + jnp.asarray(neutral, value.dtype)

    def hop(position, subtotal):
        longer = join(subtotal, pieces[position])
        return jnp.where(position < mine, longer, subtotal)

    return lax.fori_loop(0, count - 1, hop, subtotal)


def normalize(features, norm_gain):
    widened = features.astype(jnp.float32)
    mean_square = jnp.mean(widened * widened, axis=1, keepdims=True)
    return (
        widened * lax.rsqrt(mean_square + epsilon) * norm_gain.astype(jnp.float32)[None, :]
    ).astype(jnp.bfloat16)


def add_terms(earlier, latter):
    return earlier + latter


def local(hidden, norm_gain, head_weight, floor_counts, totals, targets):
    vocab_width = head_weight.shape[1]
    gathered = lax.all_gather(hidden, "tensor", axis=1, tiled=True)
    normed = normalize(gathered, norm_gain)
    logits = jnp.dot(
        lax.all_gather(normed, "stream", axis=0, tiled=True),
        head_weight,
        preferred_element_type=jnp.float32,
    )
    local_peak = jnp.max(logits, axis=1)
    floor_float = floor_counts.astype(jnp.float32)
    floor_local = jnp.sum(floor_float)
    token_total = totals.astype(jnp.float32)
    position = lax.axis_index(("stream", "tensor"))
    column_ids = position * vocab_width + jnp.arange(vocab_width, dtype=jnp.int32)
    target_hit = column_ids[None, :] == targets[:, None]
    row_peak = lax.pmax(local_peak, ("stream", "tensor"))
    exponent = jnp.exp(logits - row_peak[:, None])
    row_mass, floor_sum = lax.psum((jnp.sum(exponent, axis=1), floor_local), ("stream", "tensor"))
    probabilities = exponent / row_mass[:, None]
    quantized = (
        floor_float[None, :] + probabilities * (token_total[:, None] - floor_sum)
    ) / token_total[:, None]
    row_sum = jnp.sum(quantized, axis=1)
    picked_local = jnp.sum(jnp.where(target_hit, quantized, 0.0), axis=1)
    offsets = prefix(row_sum, ("stream", "tensor"), add_terms, jnp.zeros_like(row_sum))
    picked = lax.psum(picked_local, ("stream", "tensor"))
    row_ids = jnp.arange(vocab_width, dtype=jnp.int32)
    upper_mask = (row_ids[:, None] < row_ids[None, :]).astype(jnp.float32)
    within = jnp.dot(quantized, upper_mask, precision=lax.Precision.HIGHEST)
    cumulative = offsets[:, None] + within
    code_bits = -jnp.log2(picked)
    return (cumulative, code_bits)


def solution(mesh):
    in_specs = (
        P("stream", "tensor"),
        P(),
        P(None, ("stream", "tensor")),
        P(("stream", "tensor")),
        P(),
        P(),
    )
    out_specs = (P(None, ("stream", "tensor")), P())
    return jax.shard_map(local, mesh=mesh, in_specs=in_specs, out_specs=out_specs, check_vma=False)
```

profile of v0, /device:TPU:27, one launch (start us, length us, event | category | flops | bytes accessed | tf_op | source)
XLA Modules:
  0.0 437.5 jit_solution(16804986860595109017)
XLA Ops:
  7.2 0.0 all-gather.5.cloned.1.call-start
  7.2 0.7 all-gather.5.cloned.1.call-update
  7.9 0.0 all-gather.7.cloned.1.call-start
  7.9 0.7 convert_element_type.18
  8.7 19.0 %all-gather.5.cloned.1.call-done = bf16[64,8192]{1,0:T(8,128)(2,1)} async-done(((bf16[64,2048]{1,0:T(8,128)(2,1)}), bf16[64,8192]{1,0:T(8,128)(2,1)}) %all-gather.5.cloned.1.call-update) | async-done | bytes 1048592 | tf_op jit(solution)/shard_map/all_gather | solution.py:35
  27.7 1.5 fusion.3
  29.2 2.5 fusion.5
  31.7 0.0 all-gather.7.cloned.1.call-update
  31.8 0.7 convert_element_type.16
  32.5 1.3 convert_reduce_fusion
  33.8 11.8 %iota_compare_fusion.6 = pred[4008,4008]{1,0:T(8,128)(4,1)} fusion(), kind=kLoop, calls=%fused_computation.2.clone.clone.clone.clone.1 | loop fusion | flops 16064064 | bytes 16064064 | tf_op jit(solution)/shard_map/dot_general | solution.py:62
  45.6 108.1 %all-gather.7.cloned.1.call-done = bf16[512,8192]{1,0:T(8,128)(2,1)} async-done(((bf16[64,8192]{1,0:T(8,128)(2,1)}), bf16[512,8192]{1,0:T(8,128)(2,1)}) %all-gather.7.cloned.1.call-update) | async-done | bytes 8388624 | tf_op jit(solution)/shard_map/all_gather | solution.py:38
  153.7 43.0 %fusion.6 = (f32[512]{0:T(512)S(1)}, f32[512,4008]{0,1:T(8,128)}) fusion(bf16[512,8192]{1,0:T(8,128)(2,1)} %all-gather.7.cloned.1.call-done, bf16[8192,4008]{0,1:T(8,128)(2,1)} %param.10), kind=kOutput, calls=%fused_computation.20 | convolution fusion | flops 33623592960 | bytes 82266112 | tf_op jit(solution)/shard_map/dot_general | solution.py:37
  196.7 0.0 copy-start
  196.7 0.0 copy-start.1
  196.7 40.1 %pmax.7 = f32[512]{0:T(512)S(1)} all-reduce(f32[512]{0:T(512)S(1)} %get-tuple-element.110), channel_id=1, replica_groups=mesh['stream'=8,'tensor'=4] {'stream','tensor'}, use_global_device_ids=true, to_apply=%region_2.0 | all-reduce | flops 512 | bytes 4096 | tf_op jit(solution)/shard_map/pmax | solution.py:49
  236.8 4.5 %fusion.1 = f32[512]{0:T(512)S(1)} fusion(f32[512,4008]{0,1:T(8,128)} %get-tuple-element.111, f32[512]{0:T(512)S(1)} %pmax.7), kind=kLoop, calls=%fused_computation.7 | loop fusion | flops 4103680 | bytes 8212480 | tf_op jit(solution)/shard_map/reduce_sum | solution.py:51
  241.2 0.0 copy-done
  241.3 39.6 %all-reduce = (f32[]{:T(128)}, f32[512]{0:T(512)S(1)}) all-reduce(f32[]{:T(128)} %convert_reduce_fusion, f32[512]{0:T(512)S(1)} %fusion.1), channel_id=1, replica_groups=mesh['stream'=8,'tensor'=4] {'stream','tensor'}, use_global_device_ids=true, to_apply=%region_6.0 | all-reduce | flops 513 | bytes 4104 | tf_op jit(solution)/shard_map/psum | solution.py:51
  280.8 0.6 broadcast_subtract_fusion
  281.5 0.0 copy-done.1
  281.5 9.9 %select_reduce_fusion = (f32[512]{0:T(512)S(1)}, f32[512]{0:T(512)S(1)}, f32[512,4008]{0,1:T(8,128)}) fusion(s32[512]{0:T(512)S(1)} %copy-done.1, s32[4008]{0:T(1024)S(1)} %iota_add_fusion, f32[512]{0:T(512)S(1)} %convert_element_type.20, f32[512]{0:T(512)S(1)} %broadcast_subtract_fusion, f32[512]{0:T(512)S(1)} %get-tuple-element.108, ...), kind=kLoop, calls=%fused_computation.4 | loop fusion | flops 18467840 | bytes 16463168 | tf_op jit(solution)/shard_map/reduce_sum | solution.py:57
  291.4 40.9 %psum.23 = f32[512]{0:T(512)S(1)} all-reduce(f32[512]{0:T(512)S(1)} %get-tuple-element.97), channel_id=1, replica_groups=mesh['stream'=8,'tensor'=4] {'stream','tensor'}, use_global_device_ids=true, to_apply=%region_11.12 | all-reduce | flops 512 | bytes 4096 | tf_op jit(solution)/shard_map/psum | solution.py:59
  332.3 0.6 multiply_negate_fusion
  332.9 36.5 %all-gather.1 = f32[32,1,512]{2,1,0:T(1,128)S(1)} all-gather(f32[1,1,512]{2,1,0:T(1,128)S(1)} %bitcast.14), channel_id=2, replica_groups=mesh['stream'=8,'tensor'=4] {'stream','tensor'}, dimensions={0}, use_global_device_ids=true | all-gather | bytes 67584 | tf_op jit(solution)/shard_map/all_gather | solution.py:11
  369.4 1.7 while.14
  371.1 59.5 %fusion.2 = f32[512,4008]{0,1:T(8,128)} fusion(f32[512,4008]{0,1:T(8,128)} %get-tuple-element.109, f32[512]{0:T(512)S(1)} %get-tuple-element.81, pred[4008,4008]{1,0:T(8,128)(4,1)} %iota_compare_fusion.6), kind=kOutput, calls=%fused_computation.8 | convolution fusion | flops 98699657216 | bytes 32482880 | tf_op jit(solution)/shard_map/dot_general | solution.py:62
  (67 shorter events, 0.7 us)
Async XLA Ops:
  7.2 20.5 %all-gather.5.cloned.1.call-start = ((), (), s32[]{:S(2)}) async-start(), calls=%async_computation | async-start | bytes 1310720 | tf_op jit(solution)/shard_map/all_gather | solution.py:35
  7.9 145.8 %all-gather.7.cloned.1.call-start = ((), (), s32[]{:S(2)}) async-start(), calls=%async_computation.1 | async-start | bytes 9437184 | tf_op jit(solution)/shard_map/all_gather | solution.py:38
  196.7 44.6 %copy-start = (s32[512]{0:T(512)S(1)}, s32[512]{0:T(512)}, u32[]{:S(2)}) copy-start(s32[512]{0:T(512)} %param.12) | copy-start | bytes 6148
  196.7 84.8 %copy-start.1 = (s32[512]{0:T(512)S(1)}, s32[512]{0:T(512)}, u32[]{:S(2)}) copy-start(s32[512]{0:T(512)} %param.13) | copy-start | bytes 6148
Sparse Core Ops, SparseCore 0:
  9.6 18.0 all-gather.4
  31.9 121.8 all-gather.6
where the time goes:
time: 446 us; the launch traced here: 437 us
  blocking collectives  157 us (35%)
  waiting for transfers between devices  128 us (29%)
  matrix products  102 us (23%)
  other arithmetic  34.6 us (8%)
  between operations  14.1 us (3%)
    all_gather x1, waiting for transfers between devices, local(): lax.all_gather(normed, 'stream', axis=0, tiled=True)  108 us
    dot_general x1, matrix products, local(): within = jnp.dot(quantized, upper_mask, precision=lax.Precision.HIGHEST)  59.5 us
    dot_general x1, matrix products, local(): jnp.dot(lax.all_gather(normed, 'stream', axis=0, tiled=True), head_weight...  43 us
    psum x1, blocking collectives, local(): picked = lax.psum(picked_local, ('stream', 'tensor'))  40.9 us
    pmax x1, blocking collectives, local(): row_peak = lax.pmax(local_peak, ('stream', 'tensor'))  40.1 us
    psum x1, blocking collectives, local(): lax.psum((jnp.sum(exponent, axis=1), floor_local), ('stream', 'tensor'))  39.6 us
    all_gather x1, blocking collectives, prefix(): pieces = lax.all_gather(value, axis)  36.5 us
    all_gather x1, waiting for transfers between devices, local(): gathered = lax.all_gather(hidden, 'tensor', axis=1, tiled=True)  19 us
  transfers between devices with their start and end apart: 2, of which 2 were waited for; matrix products, arithmetic and copies ran while one was open for 3% of the time, Pallas kernels for 0%

commit v1 on v0

v1 whole, which is shorter than its diff:
```python
import functools

import jax
import jax.numpy as jnp
from jax import lax
from jax.experimental import pallas as pl
from jax.experimental.pallas import tpu as pltpu
from jax.sharding import PartitionSpec as P

epsilon = 1e-05
BLOCK = 256
BOTH = ("stream", "tensor")


def blocks_of(width):
    return [(start, min(BLOCK, width - start)) for start in range(0, width, BLOCK)]


def strict_upper(size):
    row = lax.broadcasted_iota(jnp.int32, (size, size), 0)
    col = lax.broadcasted_iota(jnp.int32, (size, size), 1)
    return jnp.where(row < col, 1.0, 0.0).astype(jnp.bfloat16)


def running_sum(value, upper, emit):
    rows, width = value.shape
    total = jnp.zeros((rows, 1), jnp.float32)
    for start, size in blocks_of(width):
        piece = value[:, start : start + size]
        high = piece.astype(jnp.bfloat16)
        low = (piece - high.astype(jnp.float32)).astype(jnp.bfloat16)
        within = jnp.dot(
            jnp.concatenate([high, low], axis=0), upper[:size, :size], preferred_element_type=jnp.float32
        )
        emit(start, size, total + (within[:rows] + within[rows:]))
        total += jnp.sum(piece, axis=1, keepdims=True)
    return total


def post_kernel(logits_ref, floor_ref, target_ref, running_ref, floor_running_ref, stats_ref):
    logits = logits_ref[...]
    rows, width = logits.shape
    peak = jnp.max(logits, axis=1, keepdims=True)
    exponent = jnp.exp(logits - peak)
    hit = lax.broadcasted_iota(jnp.int32, (rows, width), 1) == target_ref[...]
    picked = jnp.sum(jnp.where(hit, exponent, 0.0), axis=1, keepdims=True)
    floor = floor_ref[...]
    floor_picked = jnp.sum(jnp.where(hit, floor[:1], 0.0), axis=1, keepdims=True)

    def emit(start, size, piece):
        running_ref[:, start : start + size] = piece

    mass = running_sum(exponent, strict_upper(BLOCK), emit)

    def emit_floor(start, size, piece):
        floor_running_ref[:, start : start + size] = piece

    floor_mass = running_sum(floor, strict_upper(BLOCK), emit_floor)
    lane = lax.broadcasted_iota(jnp.int32, stats_ref.shape, 1)
    stats = jnp.where(lane == 0, peak, 0.0)
    stats = jnp.where(lane == 1, mass, stats)
    stats = jnp.where(lane == 2, picked, stats)
    stats = jnp.where(lane == 3, floor_picked, stats)
    stats = jnp.where(lane == 4, floor_mass[:1], stats)
    stats_ref[...] = stats


def post(logits, floor, target):
    tokens, width = logits.shape
    rows = 64
    return pl.pallas_call(
        post_kernel,
        grid=(tokens // rows,),
        in_specs=[
            pl.BlockSpec((rows, width), lambda i: (i, 0)),
            pl.BlockSpec((8, width), lambda i: (0, 0)),
            pl.BlockSpec((rows, 1), lambda i: (i, 0)),
        ],
        out_specs=[
            pl.BlockSpec((rows, width), lambda i: (i, 0)),
            pl.BlockSpec((8, width), lambda i: (0, 0)),
            pl.BlockSpec((rows, 128), lambda i: (i, 0)),
        ],
        out_shape=[
            jax.ShapeDtypeStruct((tokens, width), jnp.float32),
            jax.ShapeDtypeStruct((8, width), jnp.float32),
            jax.ShapeDtypeStruct((tokens, 128), jnp.float32),
        ],
        compiler_params=pltpu.CompilerParams(vmem_limit_bytes=40 * 2**20),
        cost_estimate=pl.CostEstimate(
            flops=4 * tokens * width * BLOCK, bytes_accessed=8 * tokens * width, transcendentals=tokens * width
        ),
    )(logits, floor, target)


def finish(stats, running, floor_running, totals, mine):
    peak, mass, picked, floor_picked, floor_mass = (stats[:, i] for i in range(5))
    total = totals.astype(jnp.float32)
    row_peak = jnp.max(peak, axis=0)
    lift = jnp.exp(peak - row_peak[None])
    row_mass = jnp.sum(mass * lift, axis=0)
    floor_sum = jnp.sum(floor_mass[:, :1])
    share = (total - floor_sum) / (row_mass * total)
    scale = lift * share[None]
    block_sum = floor_mass / total[None] + mass * scale
    below = (jnp.arange(peak.shape[0]) < mine)[:, None]
    offset = jnp.sum(jnp.where(below, block_sum, 0.0), axis=0)
    target_mass = jnp.sum(floor_picked / total[None] + picked * scale, axis=0)
    my_scale = jnp.sum(jnp.where((jnp.arange(peak.shape[0]) == mine)[:, None], scale, 0.0), axis=0)
    cumulative = offset[:, None] + floor_running[:1] * (1.0 / total)[:, None] + running * my_scale[:, None]
    return cumulative, -jnp.log2(target_mass)


def local(hidden, norm_gain, head_weight, floor_counts, totals, targets):
    vocab_width = head_weight.shape[1]
    mine = lax.axis_index(BOTH)
    depth = hidden.shape[1]
    widened = hidden.astype(jnp.float32)
    square = lax.psum(jnp.sum(widened * widened, axis=1, keepdims=True), "tensor")
    mean_square = square / (depth * lax.axis_size("tensor"))
    gain = lax.dynamic_slice(norm_gain, (lax.axis_index("tensor") * depth,), (depth,))
    normed = (widened * lax.rsqrt(mean_square + epsilon) * gain.astype(jnp.float32)[None, :]).astype(jnp.bfloat16)
    normed = lax.all_gather(normed, "tensor", axis=1, tiled=True)
    normed = lax.all_gather(normed, "stream", axis=0, tiled=True)
    logits = jnp.dot(normed, head_weight, preferred_element_type=jnp.float32)
    floor = jnp.broadcast_to(floor_counts.astype(jnp.float32)[None, :], (8, vocab_width))
    target = (targets - mine * vocab_width)[:, None]
    running, floor_running, stats = post(logits, floor, target)
    stats = lax.all_gather(stats[:, :8].T, BOTH)
    return finish(stats, running, floor_running, totals, mine)


MESH = pl.DeviceIdType.MESH
PARTS = 4
SLOTS = 8
TILE = 1024


def head_kernel(
    devices, hidden_ref, gain_ref, weight_ref, floor_ref, target_ref, total_ref,
    running_ref, floor_running_ref, scales_ref, bits_ref,
    acts, acc, weights, upper, squares, stats, columns,
    square_send, square_recv, line_send, line_recv, first_send, first_recv,
    second_send, second_recv, pair_send, pair_recv, stats_send, stats_recv, weight_sem, out_sem,
):
    rows, depth = hidden_ref.shape
    tokens, width = acc.shape
    part = depth // PARTS
    deep = acts.shape[0] // PARTS
    line = tokens // rows // 2
    stream, tensor = lax.axis_index("stream"), lax.axis_index("tensor")
    place, side = stream // 2, stream % 2
    level, core = tensor // 2, tensor % 2
    me = stream * deep + tensor
    first_side, first_level = (side + core) % 2, (level + 1 - core) % 2
    second_side, second_level = (side + 1 - core) % 2, (level + core) % 2
    far_level = (level + 1) % 2
    first_to = (place * 2 + first_side, first_level * 2 + core)
    second_to = (place * 2 + second_side, second_level * 2 + core)
    pair_to = (stream, level * 2 + 1 - core)

    barrier = pltpu.get_barrier_semaphore()

    def greet(step, carry):
        other = (me + step) % devices
        pl.semaphore_signal(barrier, inc=1, device_id=(other // deep, other % deep), device_id_type=MESH)
        return carry

    lax.fori_loop(1, devices, greet, 0)

    def chunk_of(step):
        turn, kind = step // 4, step % 4
        at_level = (level + kind % 2) % 2
        at_core = (core + kind // 2) % 2
        return (at_level * 2 + at_core) * PARTS + turn

    def weight_copy(step):
        start = pl.multiple_of(chunk_of(step) * part, part)
        slot = step % SLOTS
        return pltpu.make_async_copy(weight_ref.at[pl.ds(start, part), :], weights.at[slot], weight_sem.at[slot])

    steps = deep * PARTS

    def first_weights(step, carry):
        weight_copy(step).start()
        return carry

    lax.fori_loop(0, SLOTS, first_weights, 0)

    def block(at_place, at_side, at_tensor, turn):
        start = pl.multiple_of((at_place * 2 + at_side) * rows, rows)
        return acts.at[at_tensor * PARTS + turn, pl.ds(start, rows), :]

    def send(ref, send_sem, recv_sem, to):
        return pltpu.make_async_remote_copy(
            src_ref=ref, dst_ref=ref, send_sem=send_sem, recv_sem=recv_sem, device_id=to, device_id_type=MESH
        )

    def line_copy(at_place, turn, to_place):
        return send(
            block(at_place, side, tensor, turn),
            line_send.at[turn, to_place], line_recv.at[turn, at_place], (to_place * 2 + side, tensor),
        )

    def first_copy(at_place, at_side, at_level, turn):
        return send(
            block(at_place, at_side, at_level * 2 + core, turn),
            first_send.at[turn, at_place], first_recv.at[turn, at_place], first_to,
        )

    def second_copy(at_place, at_side, at_level, turn, index):
        return send(
            block(at_place, at_side, at_level * 2 + core, turn),
            second_send.at[turn, index], second_recv.at[turn, index], second_to,
        )

    def pair_copy(at_tensor, turn, index):
        return send(
            acts.at[at_tensor * PARTS + turn], pair_send.at[turn, index], pair_recv.at[turn, index], pair_to
        )

    hidden = hidden_ref[...].astype(jnp.float32)
    squares[tensor] = jnp.broadcast_to(jnp.sum(hidden * hidden, axis=1, keepdims=True), squares.shape[1:])
    pl.semaphore_wait(barrier, devices - 1)

    def square_copy(of, to):
        return send(squares.at[of], square_send.at[to], square_recv.at[of], (stream, to))

    for step in range(1, deep):
        square_copy(tensor, (tensor + step) % deep).start()

    row = lax.broadcasted_iota(jnp.int32, upper.shape, 0)
    col = lax.broadcasted_iota(jnp.int32, upper.shape, 1)
    upper[...] = jnp.where(row < col, 1.0, 0.0).astype(jnp.bfloat16)
    acc[...] = jnp.zeros_like(acc)
    for step in range(1, deep):
        square_copy((tensor + step) % deep, tensor).wait_recv()
    square = jnp.sum(squares[...], axis=0)[:, :1]
    factor = lax.rsqrt(square / (depth * deep) + epsilon)
    for turn in range(PARTS):
        at = slice(turn * part, (turn + 1) * part)
        gain = gain_ref[pl.ds(tensor, 1), at].astype(jnp.float32)
        normed = hidden_ref[:, at].astype(jnp.float32) * factor * gain
        start = pl.multiple_of(stream * rows, rows)
        acts[tensor * PARTS + turn, pl.ds(start, rows), :] = normed.astype(jnp.bfloat16)
        for step in range(1, line):
            line_copy(place, turn, (place + step) % line).start()
        first_copy(place, side, level, turn).start()
        second_copy(place, side, level, turn, place).start()

    def pass_line(turn):
        def go(step, carry):
            at = (place + step) % line
            line_copy(at, turn, place).wait_recv()
            first_copy(at, side, level, turn).start()
            second_copy(at, side, level, turn, at).start()
            return carry

        lax.fori_loop(1, line, go, 0)

    def pass_first(turn):
        def go(step, carry):
            at = (place + step) % line
            first_copy(at, first_side, first_level, turn).wait_recv()
            second_copy(at, first_side, first_level, turn, line + at).start()
            return carry

        lax.fori_loop(0, line, go, 0)

    def pass_second(turn):
        def go(step, carry):
            at = (place + step) % line
            second_copy(at, second_side, second_level, turn, at).wait_recv()
            return carry

        def go_far(step, carry):
            at = (place + step) % line
            second_copy(at, (side + 1) % 2, far_level, turn, line + at).wait_recv()
            return carry

        lax.fori_loop(0, line, go, 0)
        lax.fori_loop(0, line, go_far, 0)
        pair_copy(tensor, turn, 0).start()
        pair_copy(far_level * 2 + core, turn, 1).start()

    pass_line(0)
    pass_first(0)
    pass_line(1)
    pass_second(0)

    def multiply(step, carry):
        turn, kind = step // 4, step % 4

        @pl.when((kind == 0) & (turn + 2 < PARTS))
        def _():
            pass_line(turn + 2)

        @pl.when((kind == 0) & (turn + 1 < PARTS))
        def _():
            pass_first(turn + 1)

        @pl.when(kind == 2)
        def _():
            pair_copy(level * 2 + 1 - core, turn, 0).wait_recv()
            pair_copy(far_level * 2 + 1 - core, turn, 1).wait_recv()

        weight_copy(step).wait()
        chunk, slot = chunk_of(step), step % SLOTS
        for start in range(0, width, TILE):
            at = slice(start, min(start + TILE, width))
            acc[:, at] += jnp.dot(acts[chunk], weights[slot, :, at], preferred_element_type=jnp.float32)

        @pl.when(step + SLOTS < steps)
        def _():
            weight_copy(step + SLOTS).start()

        @pl.when((kind == 3) & (turn + 1 < PARTS))
        def _():
            pass_second(turn + 1)

        return carry

    lax.fori_loop(0, steps, multiply, 0)

    floor = floor_ref[...]
    floor_mass = jnp.sum(floor[:1], axis=1, keepdims=True)
    small = 32

    def measure(step, carry):
        at = pl.ds(pl.multiple_of(step * small, small), small)
        logits = acc[at, :]
        peak = jnp.max(logits, axis=1, keepdims=True)
        exponent = jnp.exp(logits - peak)
        acc[at, :] = exponent
        hit = lax.broadcasted_iota(jnp.int32, (small, width), 1) == target_ref[at, :]
        picked = jnp.sum(jnp.where(hit, exponent, 0.0), axis=1, keepdims=True)
        floor_picked = jnp.sum(jnp.where(hit, floor_ref[:1, :], 0.0), axis=1, keepdims=True)
        mass = jnp.sum(exponent, axis=1, keepdims=True)
        lane = lax.broadcasted_iota(jnp.int32, (small, 128), 1)
        value = jnp.where(lane == 0, peak, 0.0)
        value = jnp.where(lane == 1, mass, value)
        value = jnp.where(lane == 2, picked, value)
        value = jnp.where(lane == 3, floor_picked, value)
        columns[at, :] = jnp.where(lane == 4, floor_mass, value)
        return carry

    lax.fori_loop(0, tokens // small, measure, 0)
    stats[me] = columns[...].T[:8]

    def stats_copy(of, to):
        return send(stats.at[of], stats_send.at[to], stats_recv.at[of], (to // deep, to % deep))

    def share(step, carry):
        stats_copy(me, (me + step) % devices).start()
        return carry

    lax.fori_loop(1, devices, share, 0)

    def emit_floor(start, size, piece):
        floor_running_ref[:, start : start + size] = piece

    running_sum(floor, upper, emit_floor)
    large = 128

    def out_copy(step):
        at = pl.ds(pl.multiple_of(step * large, large), large)
        return pltpu.make_async_copy(acc.at[at, :], running_ref.at[at, :], out_sem.at[step])

    def accumulate(step, carry):
        at = pl.ds(pl.multiple_of(step * large, large), large)

        def emit(start, size, piece):
            acc[at, start : start + size] = piece

        running_sum(acc.at[at, :], upper, emit)
        out_copy(step).start()
        return carry

    lax.fori_loop(0, tokens // large, accumulate, 0)

    def settle(step, carry):
        stats_copy((me + step) % devices, me).wait_recv()
        return carry

    lax.fori_loop(1, devices, settle, 0)
    peak, mass, picked, floor_picked, floor_all = (stats[:, i, :] for i in range(5))
    total = total_ref[...].astype(jnp.float32)
    lift = jnp.exp(peak - jnp.max(peak, axis=0, keepdims=True))
    row_mass = jnp.sum(mass * lift, axis=0, keepdims=True)
    floor_sum = jnp.sum(floor_all, axis=0, keepdims=True)
    scale = lift * ((total - floor_sum) / (row_mass * total))
    device = lax.broadcasted_iota(jnp.int32, peak.shape, 0)
    block_sum = floor_all / total + mass * scale
    offset = jnp.sum(jnp.where(device < me, block_sum, 0.0), axis=0, keepdims=True)
    my_scale = jnp.sum(jnp.where(device == me, scale, 0.0), axis=0, keepdims=True)
    target_mass = jnp.sum(floor_picked / total + picked * scale, axis=0, keepdims=True)
    bits_ref[...] = -(jnp.log(target_mass) / 0.6931471805599453)
    lane = lax.broadcasted_iota(jnp.int32, (128, tokens), 0)
    value = jnp.where(lane == 0, offset, 0.0)
    value = jnp.where(lane == 1, 1.0 / total, value)
    value = jnp.where(lane == 2, my_scale, value)
    scales_ref[...] = value.T

    for step in range(1, deep):
        square_copy(tensor, (tensor + step) % deep).wait_send()

    def sent(turn, carry):
        def go_line(step, carry):
            line_copy(place, turn, (place + step) % line).wait_send()
            return carry

        def go(step, carry):
            first_copy(step, side, level, turn).wait_send()
            second_copy(step, side, level, turn, step).wait_send()
            second_copy(step, first_side, first_level, turn, line + step).wait_send()
            return carry

        lax.fori_loop(1, line, go_line, 0)
        lax.fori_loop(0, line, go, 0)
        pair_copy(tensor, turn, 0).wait_send()
        pair_copy(far_level * 2 + core, turn, 1).wait_send()
        return carry

    lax.fori_loop(0, PARTS, sent, 0)

    def stats_sent(step, carry):
        stats_copy(me, (me + step) % devices).wait_send()
        return carry

    lax.fori_loop(1, devices, stats_sent, 0)

    def out_done(step, carry):
        out_copy(step).wait()
        return carry

    lax.fori_loop(0, tokens // large, out_done, 0)


def head(hidden, gain, weight, floor, target, total):
    rows, depth = hidden.shape
    streams, deep = lax.axis_size("stream"), lax.axis_size("tensor")
    devices, line = streams * deep, streams // 2
    tokens, width = streams * rows, weight.shape[1]
    part = depth // PARTS
    vmem = pl.BlockSpec(memory_space=pltpu.VMEM)
    anywhere = pl.BlockSpec(memory_space=pl.ANY)
    dma = pltpu.SemaphoreType.DMA
    return pl.pallas_call(
        functools.partial(head_kernel, devices),
        in_specs=[vmem, vmem, anywhere, vmem, vmem, vmem],
        out_specs=[anywhere, vmem, vmem, vmem],
        out_shape=[
            jax.ShapeDtypeStruct((tokens, width), jnp.float32),
            jax.ShapeDtypeStruct((8, width), jnp.float32),
            jax.ShapeDtypeStruct((tokens, 128), jnp.float32),
            jax.ShapeDtypeStruct((1, tokens), jnp.float32),
        ],
        scratch_shapes=[
            pltpu.VMEM((deep * PARTS, tokens, part), jnp.bfloat16),
            pltpu.VMEM((tokens, width), jnp.float32),
            pltpu.VMEM((SLOTS, part, width), jnp.bfloat16),
            pltpu.VMEM((BLOCK, BLOCK), jnp.bfloat16),
            pltpu.VMEM((deep, rows, 128), jnp.float32),
            pltpu.VMEM((devices, 8, tokens), jnp.float32),
            pltpu.VMEM((tokens, 128), jnp.float32),
            dma((deep,)), dma((deep,)),
            dma((PARTS, line)), dma((PARTS, line)),
            dma((PARTS, line)), dma((PARTS, line)),
            dma((PARTS, 2 * line)), dma((PARTS, 2 * line)),
            dma((PARTS, 2)), dma((PARTS, 2)),
            dma((devices,)), dma((devices,)),
            dma((SLOTS,)), dma((tokens // 128,)),
        ],
        compiler_params=pltpu.CompilerParams(
            collective_id=0, has_side_effects=True, vmem_limit_bytes=62 * 2**20
        ),
        cost_estimate=pl.CostEstimate(
            flops=2 * tokens * depth * deep * width,
            bytes_accessed=2 * depth * deep * width + 4 * tokens * width,
            transcendentals=tokens * width,
        ),
    )(hidden, gain, weight, floor, target, total)


def finish_kernel(running_ref, floor_running_ref, scales_ref, out_ref):
    scales = scales_ref[...]
    out_ref[...] = scales[:, :1] + floor_running_ref[:1, :] * scales[:, 1:2] + running_ref[...] * scales[:, 2:3]


def finish_local(running, floor_running, scales):
    tokens, width = running.shape
    rows = 64
    tile = pl.BlockSpec((rows, width), lambda i: (i, 0))
    return pl.pallas_call(
        finish_kernel,
        grid=(tokens // rows,),
        in_specs=[tile, pl.BlockSpec((8, width), lambda i: (0, 0)), pl.BlockSpec((rows, 128), lambda i: (i, 0))],
        out_specs=tile,
        out_shape=jax.ShapeDtypeStruct((tokens, width), jnp.float32),
        compiler_params=pltpu.CompilerParams(vmem_limit_bytes=40 * 2**20),
        cost_estimate=pl.CostEstimate(flops=4 * tokens * width, bytes_accessed=8 * tokens * width, transcendentals=0),
    )(running, floor_running, scales)


def local_fused(hidden, norm_gain, head_weight, floor_counts, totals, targets):
    vocab_width = head_weight.shape[1]
    mine = lax.axis_index(BOTH)
    floor = jnp.broadcast_to(floor_counts.astype(jnp.float32)[None, :], (8, vocab_width))
    target = (targets - mine * vocab_width)[:, None]
    gain = norm_gain.astype(jnp.float32).reshape(-1, hidden.shape[1])
    running, floor_running, scales, bits = head(hidden, gain, head_weight, floor, target, totals[None, :])
    return finish_local(running, floor_running, scales), bits[0]


def solution(mesh):
    in_specs = (P("stream", "tensor"), P(), P(None, BOTH), P(BOTH), P(), P())
    out_specs = (P(None, BOTH), P())
    fused = mesh.shape["tensor"] == 4 and mesh.shape["stream"] % 2 == 0 and mesh.shape["stream"] <= 8
    body = local_fused if fused else local
    return jax.shard_map(body, mesh=mesh, in_specs=in_specs, out_specs=out_specs, check_vma=False)
```

time: 446 us -> 202 us (0.45); the launches traced: 437 us -> 199 us
  blocking collectives: 157 us -> 0 us
  waiting for transfers between devices: 128 us -> 0 us
  matrix products: 102 us -> 0 us
  Pallas kernels: 0 us -> 99.7 us
  local copies, waits for them, and re-layouts: 0.32 us -> 97.4 us
  other arithmetic: 34.6 us -> 1.41 us
  between operations: 14.1 us -> 0.67 us
    all_gather x2 -> x0, waiting for transfers between devices: 127 us -> none  [the longest x1 108 us: local(): lax.all_gather(normed, 'stream', axis=0, tiled=True)]
    dot_general x2 -> x0, matrix products: 102 us -> none  [the longest x1 59.5 us: local(): within = jnp.dot(quantized, upper_mask, precision=lax.Precision.HIGHEST)]
    pallas_call x0 -> x2, Pallas kernels: none -> 99.7 us  [the longest x1 93.1 us: head(): pl.pallas_call(functools.partial(head_kernel, devices), in_specs=[vmem, v...]
    unnamed x5 -> x11, local copies, waits for them, and re-layouts: 0.01 us -> 94.5 us
    psum x2 -> x0, blocking collectives: 80.4 us -> none  [the longest x1 40.9 us: local(): picked = lax.psum(picked_local, ('stream', 'tensor'))]
    pmax x1 -> x0, blocking collectives: 40.1 us -> none  [local(): row_peak = lax.pmax(local_peak, ('stream', 'tensor'))]
    all_gather x1 -> x0, blocking collectives: 36.5 us -> none  [prefix(): pieces = lax.all_gather(value, axis)]
    reduce_sum x4 -> x0, other arithmetic: 17.2 us -> none  [the longest x1 9.9 us: local(): picked_local = jnp.sum(jnp.where(target_hit, quantized, 0.0), axis=1)]
  transfers between devices with their start and end apart: 2 -> 0, of which waited for: 2 -> 0; matrix products, arithmetic and copies ran while one was open for 3% -> 0% of each run, Pallas kernels for 0% -> 0%
where the time goes in v1:
time: 202 us; the launch traced here: 199 us
  Pallas kernels  99.7 us (49%)
  local copies, waits for them, and re-layouts  97.4 us (48%)
    unnamed x11, local copies, waits for them, and re-layouts  94.5 us
    pallas_call x1, Pallas kernels, head(): pl.pallas_call(functools.partial(head_kernel, devices), in_specs=[vmem, v...  93.1 us
    pallas_call x1, Pallas kernels, finish_local(): pl.pallas_call(finish_kernel, grid=(tokens // rows,), in_specs=[tile, pl....  6.6 us

profile of v1, /device:TPU:27, one launch (start us, length us, event | category | flops | bytes accessed | tf_op | source)
XLA Modules:
  0.0 199.2 jit_solution(9421702717358380375)
XLA Ops:
  0.6 0.7 broadcast_subtract_fusion
  1.3 0.7 convert_element_type.4
  2.0 1.3 reshape.13.gain_ref
  3.4 0.7 broadcast_in_dim.12.floor_ref
  4.0 0.9 copy.11.target_ref
  4.9 80.0 %copy.10.weight_ref = bf16[8192,4008]{1,0:T(8,128)(2,1)} copy(bf16[8192,4008]{0,1:T(8,128)(2,1)} %param.8) | data formatting | bytes 131334144 | tf_op args[2]
  84.9 93.1 %shard_map.77 = (f32[512,4008]{1,0:T(8,128)}, f32[8,4008]{1,0:T(8,128)}, f32[512,128]{1,0:T(8,128)}, f32[1,512]{1,0:T(1,128)}) custom-call(bf16[64,2048]{1,0:T(8,128)(2,1)} %hidden_ref.1, f32[4,2048]{1,0:T(4,128)} %reshape.13.gain_ref, bf16[8192,4008]{1,0:T(8,128)(2,1)} %copy.10.weight_ref, f32[8,4008]{1,0:T(8,128)} %broadcast_in_dim.12.floor_ref, ...), custom_call_target="tpu_custom_call" | custom-call | flops 33621540864 | bytes 73875456 | tf_op jit(solution)/shard_map/pallas_call | solution.py:448
  178.0 0.0 copy-start.1
  178.0 0.9 copy-done.1
  179.0 0.0 copy-start.2
  179.0 0.9 copy-done.2
  179.9 6.6 %shard_map.78 = f32[512,4008]{1,0:T(8,128)S(1)} custom-call(f32[512,4008]{1,0:T(8,128)} %get-tuple-element.6.running_ref, f32[8,4008]{1,0:T(8,128)S(1)} %copy-done.2, f32[512,128]{1,0:T(8,128)S(1)} %copy-done.1), custom_call_target="tpu_custom_call" | custom-call | flops 8208384 | bytes 16416768 | tf_op jit(solution)/shard_map/pallas_call | solution.py:494
  186.5 0.0 copy-start
  186.5 3.2 %copy-done = f32[512,4008]{1,0:T(8,128)} copy-done((f32[512,4008]{1,0:T(8,128)}, f32[512,4008]{1,0:T(8,128)S(1)}, u32[]{:S(2)}) %copy-start) | copy-done | bytes 8208408
  189.7 0.0 copy-start.3
  189.7 8.9 %copy.12 = f32[512,4008]{0,1:T(8,128)} copy(f32[512,4008]{1,0:T(8,128)} %copy-done) | data formatting | bytes 16416768
  198.6 0.0 copy-done.3
  198.6 0.6 copy.14
Async XLA Ops:
  178.0 1.0 copy-start.1
  179.0 0.9 copy-start.2
  186.5 3.2 %copy-start = (f32[512,4008]{1,0:T(8,128)}, f32[512,4008]{1,0:T(8,128)S(1)}, u32[]{:S(2)}) copy-start(f32[512,4008]{1,0:T(8,128)S(1)} %shard_map.78) | copy-start | bytes 24625156
  189.7 8.9 %copy-start.3 = (f32[1,512]{1,0:T(1,128)S(1)}, f32[1,512]{1,0:T(1,128)}, u32[]{:S(2)}) copy-start(f32[1,512]{1,0:T(1,128)} %get-tuple-element.9) | copy-start | bytes 6148

commit v2 on v1

--- a/solution.py
+++ b/solution.py
@@ -136,15 +136,19 @@
 TILE = 1024
 
 
+def product(left, right):
+    return lax.dot_general(left, right, (((1,), (1,)), ((), ())), preferred_element_type=jnp.float32)
+
+
 def head_kernel(
     devices, hidden_ref, gain_ref, weight_ref, floor_ref, target_ref, total_ref,
     running_ref, floor_running_ref, scales_ref, bits_ref,
-    acts, acc, weights, upper, squares, stats, columns,
+    acts, acc, weights, lower, squares, stats, floors,
     square_send, square_recv, line_send, line_recv, first_send, first_recv,
     second_send, second_recv, pair_send, pair_recv, stats_send, stats_recv, weight_sem, out_sem,
 ):
     rows, depth = hidden_ref.shape
-    tokens, width = acc.shape
+    width, tokens = acc.shape
     part = depth // PARTS
     deep = acts.shape[0] // PARTS
     line = tokens // rows // 2
@@ -177,7 +181,7 @@
     def weight_copy(step):
         start = pl.multiple_of(chunk_of(step) * part, part)
         slot = step % SLOTS
-        return pltpu.make_async_copy(weight_ref.at[pl.ds(start, part), :], weights.at[slot], weight_sem.at[slot])
+        return pltpu.make_async_copy(weight_ref.at[:, pl.ds(start, part)], weights.at[slot], weight_sem.at[slot])
 
     steps = deep * PARTS
 
@@ -229,17 +233,13 @@
     for step in range(1, deep):
         square_copy(tensor, (tensor + step) % deep).start()
 
-    row = lax.broadcasted_iota(jnp.int32, upper.shape, 0)
-    col = lax.broadcasted_iota(jnp.int32, upper.shape, 1)
-    upper[...] = jnp.where(row < col, 1.0, 0.0).astype(jnp.bfloat16)
-    acc[...] = jnp.zeros_like(acc)
     for step in range(1, deep):
         square_copy((tensor + step) % deep, tensor).wait_recv()
     square = jnp.sum(squares[...], axis=0)[:, :1]
     factor = lax.rsqrt(square / (depth * deep) + epsilon)
     for turn in range(PARTS):
         at = slice(turn * part, (turn + 1) * part)
-        gain = gain_ref[pl.ds(tensor, 1), at].astype(jnp.float32)
+        gain = gain_ref[:, pl.ds(pl.multiple_of(tensor * depth + turn * part, part), part)]
         normed = hidden_ref[:, at].astype(jnp.float32) * factor * gain
         start = pl.multiple_of(stream * rows, rows)
         acts[tensor * PARTS + turn, pl.ds(start, rows), :] = normed.astype(jnp.bfloat16)
@@ -284,12 +284,30 @@
         pair_copy(far_level * 2 + core, turn, 1).start()
 
     pass_line(0)
+    half = acc.shape[0] // 2 // 8 * 8
+    row = lax.broadcasted_iota(jnp.int32, (BLOCK, BLOCK), 0)
+    col = lax.broadcasted_iota(jnp.int32, (BLOCK, BLOCK), 1)
+    lower[...] = jnp.where(col < row, 1.0, 0.0).astype(jnp.bfloat16)
+    acc[:half] = jnp.zeros_like(acc[:half])
     pass_first(0)
+    acc[half:] = jnp.zeros_like(acc[half:])
     pass_line(1)
+    floor_total = jnp.zeros((1, 1), jnp.float32)
+    for start, size in blocks_of(width):
+        at = slice(start, start + size)
+        piece = floor_ref[:, at].astype(jnp.float32)
+        row = lax.broadcasted_iota(jnp.int32, (size, size), 0)
+        col = lax.broadcasted_iota(jnp.int32, (size, size), 1)
+        own = jnp.sum(jnp.where(row == col, piece, 0.0), axis=1, keepdims=True)
+        below = jnp.sum(jnp.where(col < row, piece, 0.0), axis=1, keepdims=True)
+        floors[at, :] = jnp.broadcast_to(own, (size, 128))
+        floor_running_ref[at, :] = jnp.broadcast_to(floor_total + below, (size, 128))
+        floor_total += jnp.sum(piece, axis=1, keepdims=True)
     pass_second(0)
 
-    def multiply(step, carry):
-        turn, kind = step // 4, step % 4
+    def multiply(pair, carry):
+        turn, kind = pair // 2, pair % 2
+        step = 2 * pair
 
         @pl.when((kind == 0) & (turn + 2 < PARTS))
         def _():
@@ -299,53 +317,66 @@
         def _():
             pass_first(turn + 1)
 
-        @pl.when(kind == 2)
+        @pl.when(kind == 1)
         def _():
             pair_copy(level * 2 + 1 - core, turn, 0).wait_recv()
             pair_copy(far_level * 2 + 1 - core, turn, 1).wait_recv()
 
         weight_copy(step).wait()
-        chunk, slot = chunk_of(step), step % SLOTS
+        weight_copy(step + 1).wait()
+        near, far = chunk_of(step), chunk_of(step + 1)
+        slot = step % SLOTS
         for start in range(0, width, TILE):
             at = slice(start, min(start + TILE, width))
-            acc[:, at] += jnp.dot(acts[chunk], weights[slot, :, at], preferred_element_type=jnp.float32)
+            acc[at, :] += product(weights[slot, at, :], acts[near]) + product(weights[slot + 1, at, :], acts[far])
 
         @pl.when(step + SLOTS < steps)
         def _():
             weight_copy(step + SLOTS).start()
-
-        @pl.when((kind == 3) & (turn + 1 < PARTS))
+            weight_copy(step + SLOTS + 1).start()
+
+        @pl.when((kind == 1) & (turn + 1 < PARTS))
         def _():
             pass_second(turn + 1)
 
         return carry
 
-    lax.fori_loop(0, steps, multiply, 0)
-
-    floor = floor_ref[...]
-    floor_mass = jnp.sum(floor[:1], axis=1, keepdims=True)
-    small = 32
-
-    def measure(step, carry):
-        at = pl.ds(pl.multiple_of(step * small, small), small)
-        logits = acc[at, :]
-        peak = jnp.max(logits, axis=1, keepdims=True)
-        exponent = jnp.exp(logits - peak)
+    lax.fori_loop(0, steps // 2, multiply, 0)
+
+    whole, rest = width // BLOCK, width % BLOCK
+
+    def over_blocks(go, carry):
+        def body(step, carry):
+            return go(pl.multiple_of(step * BLOCK, BLOCK), BLOCK, step, carry)
+
+        carry = lax.fori_loop(0, whole, body, carry)
+        return go(whole * BLOCK, rest, whole, carry) if rest else carry
+
+    def highest(start, size, step, carry):
+        return jnp.maximum(carry, jnp.max(acc[pl.ds(start, size), :], axis=0, keepdims=True))
+
+    peak = over_blocks(highest, jnp.full((1, tokens), -jnp.inf, jnp.float32))
+    aim = target_ref[...] - me * width
+
+    def measure(start, size, step, carry):
+        mass, picked, floor_picked = carry
+        at = pl.ds(start, size)
+        exponent = jnp.exp(acc[at, :] - peak)
         acc[at, :] = exponent
-        hit = lax.broadcasted_iota(jnp.int32, (small, width), 1) == target_ref[at, :]
-        picked = jnp.sum(jnp.where(hit, exponent, 0.0), axis=1, keepdims=True)
-        floor_picked = jnp.sum(jnp.where(hit, floor_ref[:1, :], 0.0), axis=1, keepdims=True)
-        mass = jnp.sum(exponent, axis=1, keepdims=True)
-        lane = lax.broadcasted_iota(jnp.int32, (small, 128), 1)
-        value = jnp.where(lane == 0, peak, 0.0)
-        value = jnp.where(lane == 1, mass, value)
-        value = jnp.where(lane == 2, picked, value)
-        value = jnp.where(lane == 3, floor_picked, value)
-        columns[at, :] = jnp.where(lane == 4, floor_mass, value)
-        return carry
-
-    lax.fori_loop(0, tokens // small, measure, 0)
-    stats[me] = columns[...].T[:8]
+        hit = lax.broadcasted_iota(jnp.int32, (size, tokens), 0) + start == aim
+        mass += jnp.sum(exponent, axis=0, keepdims=True)
+        picked += jnp.sum(jnp.where(hit, exponent, 0.0), axis=0, keepdims=True)
+        floor_picked += jnp.sum(jnp.where(hit, floors[at, :1], 0.0), axis=0, keepdims=True)
+        return mass, picked, floor_picked
+
+    zero = jnp.zeros((1, tokens), jnp.float32)
+    mass, picked, floor_picked = over_blocks(measure, (zero, zero, zero))
+    lane = lax.broadcasted_iota(jnp.int32, (8, tokens), 0)
+    value = jnp.where(lane == 0, peak, 0.0)
+    value = jnp.where(lane == 1, mass, value)
+    value = jnp.where(lane == 2, picked, value)
+    value = jnp.where(lane == 3, floor_picked, value)
+    stats[me] = jnp.where(lane == 4, floor_total, value)
 
     def stats_copy(of, to):
         return send(stats.at[of], stats_send.at[to], stats_recv.at[of], (to // deep, to % deep))
@@ -356,27 +387,22 @@
 
     lax.fori_loop(1, devices, share, 0)
 
-    def emit_floor(start, size, piece):
-        floor_running_ref[:, start : start + size] = piece
-
-    running_sum(floor, upper, emit_floor)
-    large = 128
-
-    def out_copy(step):
-        at = pl.ds(pl.multiple_of(step * large, large), large)
+    def out_copy(start, size, step):
+        at = pl.ds(start, size)
         return pltpu.make_async_copy(acc.at[at, :], running_ref.at[at, :], out_sem.at[step])
 
-    def accumulate(step, carry):
-        at = pl.ds(pl.multiple_of(step * large, large), large)
-
-        def emit(start, size, piece):
-            acc[at, start : start + size] = piece
-
-        running_sum(acc.at[at, :], upper, emit)
-        out_copy(step).start()
-        return carry
-
-    lax.fori_loop(0, tokens // large, accumulate, 0)
+    def accumulate(start, size, step, total):
+        at = pl.ds(start, size)
+        piece = acc[at, :]
+        high = piece.astype(jnp.bfloat16)
+        low = (piece - high.astype(jnp.float32)).astype(jnp.bfloat16)
+        within = jnp.dot(lower[:size, :size], high, preferred_element_type=jnp.float32)
+        within += jnp.dot(lower[:size, :size], low, preferred_element_type=jnp.float32)
+        acc[at, :] = total + within
+        out_copy(start, size, step).start()
+        return total + jnp.sum(piece, axis=0, keepdims=True)
+
+    over_blocks(accumulate, zero)
 
     def settle(step, carry):
         stats_copy((me + step) % devices, me).wait_recv()
@@ -395,11 +421,10 @@
     my_scale = jnp.sum(jnp.where(device == me, scale, 0.0), axis=0, keepdims=True)
     target_mass = jnp.sum(floor_picked / total + picked * scale, axis=0, keepdims=True)
     bits_ref[...] = -(jnp.log(target_mass) / 0.6931471805599453)
-    lane = lax.broadcasted_iota(jnp.int32, (128, tokens), 0)
+    lane = lax.broadcasted_iota(jnp.int32, (8, tokens), 0)
     value = jnp.where(lane == 0, offset, 0.0)
     value = jnp.where(lane == 1, 1.0 / total, value)
-    value = jnp.where(lane == 2, my_scale, value)
-    scales_ref[...] = value.T
+    scales_ref[...] = jnp.where(lane == 2, my_scale, value)
 
     for step in range(1, deep):
         square_copy(tensor, (tensor + step) % deep).wait_send()
@@ -429,18 +454,18 @@
 
     lax.fori_loop(1, devices, stats_sent, 0)
 
-    def out_done(step, carry):
-        out_copy(step).wait()
-        return carry
-
-    lax.fori_loop(0, tokens // large, out_done, 0)
+    def out_done(start, size, step, carry):
+        out_copy(start, size, step).wait()
+        return carry
+
+    over_blocks(out_done, 0)
 
 
 def head(hidden, gain, weight, floor, target, total):
     rows, depth = hidden.shape
     streams, deep = lax.axis_size("stream"), lax.axis_size("tensor")
     devices, line = streams * deep, streams // 2
-    tokens, width = streams * rows, weight.shape[1]
+    tokens, width = streams * rows, weight.shape[0]
     part = depth // PARTS
     vmem = pl.BlockSpec(memory_space=pltpu.VMEM)
     anywhere = pl.BlockSpec(memory_space=pl.ANY)
@@ -450,26 +475,26 @@
         in_specs=[vmem, vmem, anywhere, vmem, vmem, vmem],
         out_specs=[anywhere, vmem, vmem, vmem],
         out_shape=[
-            jax.ShapeDtypeStruct((tokens, width), jnp.float32),
-            jax.ShapeDtypeStruct((8, width), jnp.float32),
-            jax.ShapeDtypeStruct((tokens, 128), jnp.float32),
+            jax.ShapeDtypeStruct((width, tokens), jnp.float32),
+            jax.ShapeDtypeStruct((width, 128), jnp.float32),
+            jax.ShapeDtypeStruct((8, tokens), jnp.float32),
             jax.ShapeDtypeStruct((1, tokens), jnp.float32),
         ],
         scratch_shapes=[
             pltpu.VMEM((deep * PARTS, tokens, part), jnp.bfloat16),
-            pltpu.VMEM((tokens, width), jnp.float32),
-            pltpu.VMEM((SLOTS, part, width), jnp.bfloat16),
+            pltpu.VMEM((width, tokens), jnp.float32),
+            pltpu.VMEM((SLOTS, width, part), jnp.bfloat16),
             pltpu.VMEM((BLOCK, BLOCK), jnp.bfloat16),
             pltpu.VMEM((deep, rows, 128), jnp.float32),
             pltpu.VMEM((devices, 8, tokens), jnp.float32),
-            pltpu.VMEM((tokens, 128), jnp.float32),
+            pltpu.VMEM((width, 128), jnp.float32),
             dma((deep,)), dma((deep,)),
             dma((PARTS, line)), dma((PARTS, line)),
             dma((PARTS, line)), dma((PARTS, line)),
             dma((PARTS, 2 * line)), dma((PARTS, 2 * line)),
             dma((PARTS, 2)), dma((PARTS, 2)),
             dma((devices,)), dma((devices,)),
-            dma((SLOTS,)), dma((tokens // 128,)),
+            dma((SLOTS,)), dma((len(blocks_of(width)),)),
         ],
         compiler_params=pltpu.CompilerParams(
             collective_id=0, has_side_effects=True, vmem_limit_bytes=62 * 2**20
@@ -483,33 +508,31 @@
 
 
 def finish_kernel(running_ref, floor_running_ref, scales_ref, out_ref):
-    scales = scales_ref[...]
-    out_ref[...] = scales[:, :1] + floor_running_ref[:1, :] * scales[:, 1:2] + running_ref[...] * scales[:, 2:3]
+    offset, share, scale = (scales_ref[i : i + 1, :] for i in range(3))
+    out_ref[...] = offset + floor_running_ref[:, :1] * share + running_ref[...] * scale
 
 
 def finish_local(running, floor_running, scales):
-    tokens, width = running.shape
-    rows = 64
-    tile = pl.BlockSpec((rows, width), lambda i: (i, 0))
+    width, tokens = running.shape
+    rows = 512
+    tile = pl.BlockSpec((rows, tokens), lambda i: (i, 0))
     return pl.pallas_call(
         finish_kernel,
-        grid=(tokens // rows,),
-        in_specs=[tile, pl.BlockSpec((8, width), lambda i: (0, 0)), pl.BlockSpec((rows, 128), lambda i: (i, 0))],
+        grid=(pl.cdiv(width, rows),),
+        in_specs=[tile, pl.BlockSpec((rows, 128), lambda i: (i, 0)), pl.BlockSpec((8, tokens), lambda i: (0, 0))],
         out_specs=tile,
-        out_shape=jax.ShapeDtypeStruct((tokens, width), jnp.float32),
-        compiler_params=pltpu.CompilerParams(vmem_limit_bytes=40 * 2**20),
+        out_shape=jax.ShapeDtypeStruct((width, tokens), jnp.float32),
+        compiler_params=pltpu.CompilerParams(vmem_limit_bytes=56 * 2**20),
         cost_estimate=pl.CostEstimate(flops=4 * tokens * width, bytes_accessed=8 * tokens * width, transcendentals=0),
     )(running, floor_running, scales)
 
 
 def local_fused(hidden, norm_gain, head_weight, floor_counts, totals, targets):
-    vocab_width = head_weight.shape[1]
-    mine = lax.axis_index(BOTH)
-    floor = jnp.broadcast_to(floor_counts.astype(jnp.float32)[None, :], (8, vocab_width))
-    target = (targets - mine * vocab_width)[:, None]
-    gain = norm_gain.astype(jnp.float32).reshape(-1, hidden.shape[1])
-    running, floor_running, scales, bits = head(hidden, gain, head_weight, floor, target, totals[None, :])
-    return finish_local(running, floor_running, scales), bits[0]
+    gain = norm_gain.astype(jnp.float32)[None, :]
+    running, floor_running, scales, bits = head(
+        hidden, gain, head_weight.T, floor_counts[None, :], targets[None, :], totals[None, :]
+    )
+    return finish_local(running, floor_running, scales).T, bits[0]
 
 
 def solution(mesh):

time: 202 us -> 102 us (0.50); the launches traced: 199 us -> 102 us
  local copies, waits for them, and re-layouts: 97.4 us -> 0.58 us
    unnamed x11 -> x3, local copies, waits for them, and re-layouts: 94.5 us -> 0.58 us
    pallas_call x1, Pallas kernels: 93.1 us -> 89.4 us  [head(): pl.pallas_call(functools.partial(head_kernel, devices), in_specs=[vmem, v...]
    pallas_call x1, Pallas kernels: 6.6 us -> 9.66 us  [finish_local(): pl.pallas_call(finish_kernel, grid=(pl.cdiv(width, rows),), in_specs=[til...]
where the time goes in v2:
time: 102 us
  Pallas kernels  99.1 us (97%)
  other arithmetic  1.34 us (1%)
    pallas_call x1, Pallas kernels, head(): pl.pallas_call(functools.partial(head_kernel, devices), in_specs=[vmem, v...  89.4 us
    pallas_call x1, Pallas kernels, finish_local(): pl.pallas_call(finish_kernel, grid=(pl.cdiv(width, rows),), in_specs=[til...  9.66 us

profile of v2, /device:TPU:27, one launch (start us, length us, event | category | flops | bytes accessed | tf_op | source)
XLA Modules:
  0.0 101.6 jit_solution(16683501361114662319)
XLA Ops:
  0.6 1.3 %broadcast_in_dim.19 = f32[8192]{0:T(1024)} convert(bf16[8192]{0:T(1024)(128)(2,1)} %param.7) | non-fusion elementwise | flops 8192 | bytes 49152 | tf_op jit(solution)/shard_map/broadcast_in_dim | solution.py:531
  2.0 89.4 %shard_map.77 = (f32[4008,512]{1,0:T(8,128)}, f32[4008,128]{1,0:T(8,128)}, f32[8,512]{1,0:T(8,128)}, f32[1,512]{1,0:T(1,128)}) custom-call(bf16[64,2048]{1,0:T(8,128)(2,1)} %hidden_ref.1, f32[1,8192]{1,0:T(1,128)} %bitcast.8, bf16[4008,8192]{1,0:T(8,128)(2,1)} %bitcast.10, s32[1,4008]{1,0:T(1,128)} %bitcast.11, s32[1,512]{1,0:T(1,128)} %bitcast.12, ...), custom_call_target="tpu_custom_call" | custom-call | flops 33621540864 | bytes 73875456 | tf_op jit(solution)/shard_map/pallas_call | solution.py:473
  91.4 0.0 copy-start
  91.4 9.7 %shard_map.78 = f32[4008,512]{1,0:T(8,128)} custom-call(f32[4008,512]{1,0:T(8,128)} %get-tuple-element.6.running_ref, f32[4008,128]{1,0:T(8,128)} %get-tuple-element.7.floor_running_ref, f32[8,512]{1,0:T(8,128)} %get-tuple-element.8.scales_ref), custom_call_target="tpu_custom_call" | custom-call | flops 8208384 | bytes 16416768 | tf_op jit(solution)/shard_map/pallas_call | solution.py:519
  101.1 0.0 copy-done
  101.1 0.6 copy.9
Async XLA Ops:
  91.4 9.7 %copy-start = (f32[1,512]{1,0:T(1,128)S(1)}, f32[1,512]{1,0:T(1,128)}, u32[]{:S(2)}) copy-start(f32[1,512]{1,0:T(1,128)} %get-tuple-element.9) | copy-start | bytes 6148

commit v3 on v2

--- a/solution.py
+++ b/solution.py
@@ -131,7 +131,7 @@
 
 
 MESH = pl.DeviceIdType.MESH
-PARTS = 4
+PARTS = 8
 SLOTS = 8
 TILE = 1024
 
@@ -142,10 +142,10 @@
 
 def head_kernel(
     devices, hidden_ref, gain_ref, weight_ref, floor_ref, target_ref, total_ref,
-    running_ref, floor_running_ref, scales_ref, bits_ref,
-    acts, acc, weights, lower, squares, stats, floors,
+    acc, floor_running_ref, scales_ref, bits_ref,
+    acts, weights, lower, squares, stats, floors,
     square_send, square_recv, line_send, line_recv, first_send, first_recv,
-    second_send, second_recv, pair_send, pair_recv, stats_send, stats_recv, weight_sem, out_sem,
+    second_send, second_recv, pair_send, pair_recv, stats_send, stats_recv, weight_sem,
 ):
     rows, depth = hidden_ref.shape
     width, tokens = acc.shape
@@ -191,9 +191,8 @@
 
     lax.fori_loop(0, SLOTS, first_weights, 0)
 
-    def block(at_place, at_side, at_tensor, turn):
-        start = pl.multiple_of((at_place * 2 + at_side) * rows, rows)
-        return acts.at[at_tensor * PARTS + turn, pl.ds(start, rows), :]
+    def block(at_side, at_level, turn):
+        return acts.at[(at_level * 2 + core) * PARTS + turn, at_side]
 
     def send(ref, send_sem, recv_sem, to):
         return pltpu.make_async_remote_copy(
@@ -201,21 +200,18 @@
         )
 
     def line_copy(at_place, turn, to_place):
+        start = pl.multiple_of(at_place * rows, rows)
         return send(
-            block(at_place, side, tensor, turn),
+            block(side, level, turn).at[pl.ds(start, rows), :],
             line_send.at[turn, to_place], line_recv.at[turn, at_place], (to_place * 2 + side, tensor),
         )
 
-    def first_copy(at_place, at_side, at_level, turn):
+    def first_copy(at_side, at_level, turn):
+        return send(block(at_side, at_level, turn), first_send.at[turn], first_recv.at[turn], first_to)
+
+    def second_copy(at_side, at_level, turn, index):
         return send(
-            block(at_place, at_side, at_level * 2 + core, turn),
-            first_send.at[turn, at_place], first_recv.at[turn, at_place], first_to,
-        )
-
-    def second_copy(at_place, at_side, at_level, turn, index):
-        return send(
-            block(at_place, at_side, at_level * 2 + core, turn),
-            second_send.at[turn, index], second_recv.at[turn, index], second_to,
+            block(at_side, at_level, turn), second_send.at[turn, index], second_recv.at[turn, index], second_to
         )
 
     def pair_copy(at_tensor, turn, index):
@@ -241,49 +237,29 @@
         at = slice(turn * part, (turn + 1) * part)
         gain = gain_ref[:, pl.ds(pl.multiple_of(tensor * depth + turn * part, part), part)]
         normed = hidden_ref[:, at].astype(jnp.float32) * factor * gain
-        start = pl.multiple_of(stream * rows, rows)
-        acts[tensor * PARTS + turn, pl.ds(start, rows), :] = normed.astype(jnp.bfloat16)
+        start = pl.multiple_of(place * rows, rows)
+        acts[tensor * PARTS + turn, side, pl.ds(start, rows), :] = normed.astype(jnp.bfloat16)
         for step in range(1, line):
             line_copy(place, turn, (place + step) % line).start()
-        first_copy(place, side, level, turn).start()
-        second_copy(place, side, level, turn, place).start()
 
     def pass_line(turn):
-        def go(step, carry):
-            at = (place + step) % line
-            line_copy(at, turn, place).wait_recv()
-            first_copy(at, side, level, turn).start()
-            second_copy(at, side, level, turn, at).start()
-            return carry
-
-        lax.fori_loop(1, line, go, 0)
+        for step in range(1, line):
+            line_copy((place + step) % line, turn, place).wait_recv()
+        first_copy(side, level, turn).start()
+        second_copy(side, level, turn, 0).start()
 
     def pass_first(turn):
-        def go(step, carry):
-            at = (place + step) % line
-            first_copy(at, first_side, first_level, turn).wait_recv()
-            second_copy(at, first_side, first_level, turn, line + at).start()
-            return carry
-
-        lax.fori_loop(0, line, go, 0)
+        first_copy(first_side, first_level, turn).wait_recv()
+        second_copy(first_side, first_level, turn, 1).start()
 
     def pass_second(turn):
-        def go(step, carry):
-            at = (place + step) % line
-            second_copy(at, second_side, second_level, turn, at).wait_recv()
-            return carry
-
-        def go_far(step, carry):
-            at = (place + step) % line
-            second_copy(at, (side + 1) % 2, far_level, turn, line + at).wait_recv()
-            return carry
-
-        lax.fori_loop(0, line, go, 0)
-        lax.fori_loop(0, line, go_far, 0)
+        second_copy(second_side, second_level, turn, 0).wait_recv()
+        second_copy((side + 1) % 2, far_level, turn, 1).wait_recv()
         pair_copy(tensor, turn, 0).start()
         pair_copy(far_level * 2 + core, turn, 1).start()
 
     pass_line(0)
+    pass_line(1)
     half = acc.shape[0] // 2 // 8 * 8
     row = lax.broadcasted_iota(jnp.int32, (BLOCK, BLOCK), 0)
     col = lax.broadcasted_iota(jnp.int32, (BLOCK, BLOCK), 1)
@@ -291,7 +267,8 @@
     acc[:half] = jnp.zeros_like(acc[:half])
     pass_first(0)
     acc[half:] = jnp.zeros_like(acc[half:])
-    pass_line(1)
+    pass_line(2)
+    pass_first(1)
     floor_total = jnp.zeros((1, 1), jnp.float32)
     for start, size in blocks_of(width):
         at = slice(start, start + size)
@@ -305,17 +282,21 @@
         floor_total += jnp.sum(piece, axis=1, keepdims=True)
     pass_second(0)
 
+    def states(chunk):
+        pieces = [acts[chunk, i % 2, i // 2 * rows : (i // 2 + 1) * rows, :] for i in range(2 * line)]
+        return jnp.concatenate(pieces, axis=0)
+
     def multiply(pair, carry):
         turn, kind = pair // 2, pair % 2
         step = 2 * pair
 
         @pl.when((kind == 0) & (turn + 2 < PARTS))
         def _():
-            pass_line(turn + 2)
-
-        @pl.when((kind == 0) & (turn + 1 < PARTS))
+            pass_first(turn + 2)
+
+        @pl.when((kind == 0) & (turn + 3 < PARTS))
         def _():
-            pass_first(turn + 1)
+            pass_line(turn + 3)
 
         @pl.when(kind == 1)
         def _():
@@ -328,7 +309,7 @@
         slot = step % SLOTS
         for start in range(0, width, TILE):
             at = slice(start, min(start + TILE, width))
-            acc[at, :] += product(weights[slot, at, :], acts[near]) + product(weights[slot + 1, at, :], acts[far])
+            acc[at, :] += product(weights[slot, at, :], states(near)) + product(weights[slot + 1, at, :], states(far))
 
         @pl.when(step + SLOTS < steps)
         def _():
@@ -387,10 +368,6 @@
 
     lax.fori_loop(1, devices, share, 0)
 
-    def out_copy(start, size, step):
-        at = pl.ds(start, size)
-        return pltpu.make_async_copy(acc.at[at, :], running_ref.at[at, :], out_sem.at[step])
-
     def accumulate(start, size, step, total):
         at = pl.ds(start, size)
         piece = acc[at, :]
@@ -399,7 +376,6 @@
         within = jnp.dot(lower[:size, :size], high, preferred_element_type=jnp.float32)
         within += jnp.dot(lower[:size, :size], low, preferred_element_type=jnp.float32)
         acc[at, :] = total + within
-        out_copy(start, size, step).start()
         return total + jnp.sum(piece, axis=0, keepdims=True)
 
     over_blocks(accumulate, zero)
@@ -430,18 +406,11 @@
         square_copy(tensor, (tensor + step) % deep).wait_send()
 
     def sent(turn, carry):
-        def go_line(step, carry):
+        for step in range(1, line):
             line_copy(place, turn, (place + step) % line).wait_send()
-            return carry
-
-        def go(step, carry):
-            first_copy(step, side, level, turn).wait_send()
-            second_copy(step, side, level, turn, step).wait_send()
-            second_copy(step, first_side, first_level, turn, line + step).wait_send()
-            return carry
-
-        lax.fori_loop(1, line, go_line, 0)
-        lax.fori_loop(0, line, go, 0)
+        first_copy(side, level, turn).wait_send()
+        second_copy(side, level, turn, 0).wait_send()
+        second_copy(first_side, first_level, turn, 1).wait_send()
         pair_copy(tensor, turn, 0).wait_send()
         pair_copy(far_level * 2 + core, turn, 1).wait_send()
         return carry
@@ -453,12 +422,6 @@
         return carry
 
     lax.fori_loop(1, devices, stats_sent, 0)
-
-    def out_done(start, size, step, carry):
-        out_copy(start, size, step).wait()
-        return carry
-
-    over_blocks(out_done, 0)
 
 
 def head(hidden, gain, weight, floor, target, total):
@@ -473,7 +436,7 @@
     return pl.pallas_call(
         functools.partial(head_kernel, devices),
         in_specs=[vmem, vmem, anywhere, vmem, vmem, vmem],
-        out_specs=[anywhere, vmem, vmem, vmem],
+        out_specs=[vmem, vmem, vmem, vmem],
         out_shape=[
             jax.ShapeDtypeStruct((width, tokens), jnp.float32),
             jax.ShapeDtypeStruct((width, 128), jnp.float32),
@@ -481,8 +444,7 @@
             jax.ShapeDtypeStruct((1, tokens), jnp.float32),
         ],
         scratch_shapes=[
-            pltpu.VMEM((deep * PARTS, tokens, part), jnp.bfloat16),
-            pltpu.VMEM((width, tokens), jnp.float32),
+            pltpu.VMEM((deep * PARTS, 2, line * rows, part), jnp.bfloat16),
             pltpu.VMEM((SLOTS, width, part), jnp.bfloat16),
             pltpu.VMEM((BLOCK, BLOCK), jnp.bfloat16),
             pltpu.VMEM((deep, rows, 128), jnp.float32),
@@ -490,14 +452,14 @@
             pltpu.VMEM((width, 128), jnp.float32),
             dma((deep,)), dma((deep,)),
             dma((PARTS, line)), dma((PARTS, line)),
-            dma((PARTS, line)), dma((PARTS, line)),
-            dma((PARTS, 2 * line)), dma((PARTS, 2 * line)),
+            dma((PARTS,)), dma((PARTS,)),
+            dma((PARTS, 2)), dma((PARTS, 2)),
             dma((PARTS, 2)), dma((PARTS, 2)),
             dma((devices,)), dma((devices,)),
-            dma((SLOTS,)), dma((len(blocks_of(width)),)),
+            dma((SLOTS,)),
         ],
         compiler_params=pltpu.CompilerParams(
-            collective_id=0, has_side_effects=True, vmem_limit_bytes=62 * 2**20
+            collective_id=0, has_side_effects=True, vmem_limit_bytes=42 * 2**20
         ),
         cost_estimate=pl.CostEstimate(
             flops=2 * tokens * depth * deep * width,
@@ -522,7 +484,7 @@
         in_specs=[tile, pl.BlockSpec((rows, 128), lambda i: (i, 0)), pl.BlockSpec((8, tokens), lambda i: (0, 0))],
         out_specs=tile,
         out_shape=jax.ShapeDtypeStruct((width, tokens), jnp.float32),
-        compiler_params=pltpu.CompilerParams(vmem_limit_bytes=56 * 2**20),
+        compiler_params=pltpu.CompilerParams(vmem_limit_bytes=12 * 2**20),
         cost_estimate=pl.CostEstimate(flops=4 * tokens * width, bytes_accessed=8 * tokens * width, transcendentals=0),
     )(running, floor_running, scales)
 

time: 102 us -> 97.6 us (0.957)
  Pallas kernels: 99.1 us -> 92.2 us
  local copies, waits for them, and re-layouts: 0.58 us -> 3.61 us
    pallas_call x1, Pallas kernels: 9.66 us -> 5.05 us  [finish_local(): pl.pallas_call(finish_kernel, grid=(pl.cdiv(width, rows),), in_specs=[til...]
    unnamed x3 -> x9, local copies, waits for them, and re-layouts: 0.58 us -> 3.61 us
    pallas_call x1, Pallas kernels: 89.4 us -> 87.2 us  [head(): pl.pallas_call(functools.partial(head_kernel, devices), in_specs=[vmem, v...]
where the time goes in v3:
time: 97.6 us; the launch traced here: 97.2 us
  Pallas kernels  92.2 us (94%)
  local copies, waits for them, and re-layouts  3.61 us (4%)
    pallas_call x1, Pallas kernels, head(): pl.pallas_call(functools.partial(head_kernel, devices), in_specs=[vmem, v...  87.2 us
    pallas_call x1, Pallas kernels, finish_local(): pl.pallas_call(finish_kernel, grid=(pl.cdiv(width, rows),), in_specs=[til...  5.05 us
    unnamed x9, local copies, waits for them, and re-layouts  3.61 us

profile of v3, /device:TPU:27, one launch (start us, length us, event | category | flops | bytes accessed | tf_op | source)
XLA Modules:
  0.0 97.2 jit_solution(8444877171361827895)
XLA Ops:
  0.6 0.7 broadcast_in_dim.19
  1.4 0.0 copy-start
  1.4 0.9 copy-done
  2.3 0.0 copy-start.1
  2.3 0.7 copy-done.1
  3.0 0.0 copy-start.2
  3.0 0.7 copy-done.2
  3.7 0.0 copy-start.3
  3.7 0.7 copy-done.3
  4.4 87.2 %shard_map.77 = (f32[4008,512]{1,0:T(8,128)S(1)}, f32[4008,128]{1,0:T(8,128)S(1)}, f32[8,512]{1,0:T(8,128)S(1)}, f32[1,512]{1,0:T(1,128)S(1)}) custom-call(bf16[64,2048]{1,0:T(8,128)(2,1)S(1)} %copy-done, f32[1,8192]{1,0:T(1,128)S(1)} %bitcast.7, bf16[4008,8192]{1,0:T(8,128)(2,1)} %bitcast.13, s32[1,4008]{1,0:T(1,128)S(1)} %bitcast.9, ...), custom_call_target="tpu_custom_call" | custom-call | flops 33621540864 | bytes 73875456 | tf_op jit(solution)/shard_map/pallas_call | solution.py:436
  91.6 5.0 %shard_map.78 = f32[4008,512]{1,0:T(8,128)} custom-call(f32[4008,512]{1,0:T(8,128)S(1)} %get-tuple-element.6.running_ref, f32[4008,128]{1,0:T(8,128)S(1)} %get-tuple-element.7.floor_running_ref, f32[8,512]{1,0:T(8,128)S(1)} %get-tuple-element.8.scales_ref), custom_call_target="tpu_custom_call" | custom-call | flops 8208384 | bytes 16416768 | tf_op jit(solution)/shard_map/pallas_call | solution.py:481
  96.6 0.6 copy.9
Async XLA Ops:
  1.4 0.9 copy-start
  2.3 0.7 copy-start.1
  3.0 0.7 copy-start.2
  3.7 0.7 copy-start.3
